TPU v7x, 256 devices: a whole 4x4x8 slice. The times are simulated.
256 devices in a mesh: row: 8 (over y, x_lo), col: 32 (over x_hi, z, core).
Axes of the slice: x: 4 (x_hi: 2, x_lo: 2; x = x_hi * 2 + x_lo), y: 4, z: 8, core: 2. Of those that a mesh axis runs over, the one named last changes fastest.
Arguments:
- features: bfloat16 [131072, 256], P(('row', 'col')), may hold values from -6 to 6
- weight: bfloat16 [256, 256], replicated, may hold values from -0.375 to 0.375
- cotangent: bfloat16 [131072, 256], P(('row', 'col')), may hold values from -6 to 6
- tile_rows: int32 [8, 32, 128], P('row', 'col'), may hold values from 0 to 127, as said below
- tile_cols: int32 [8, 32, 128], P('row', 'col'), may hold values from 0 to 31
- tile_values: bfloat16 [8, 32, 128, 128, 128], P('row', 'col'), may hold values from -0.09375 to 0.09375
- tile_count: int32 [8, 32], P('row', 'col'), may hold values from 32 to 128, as said below
Outputs:
- hidden: bfloat16 [131072, 256], P(('row', 'col'))
- grad_feat: bfloat16 [131072, 256], P(('row', 'col'))
- grad_weight: float32 [256, 256], replicated
Inputs may be any that keep to these rules, and one draw needn't show every extreme that they name: `tile_rows`: within one grid position the slots name distinct pairs of block row and block column. `tile_count`: some grid position uses all 128 slots and some uses 128 // 4.
All inputs are finite; a program needn't handle non-finite values.
Results may differ from a plain program's by a relative error of at most 0.018.
Values may be sent and summed in bfloat16 or wider, within the bound.
A program may use at most 192 MiB of HBM per device.

v0:
```python
import jax
import jax.numpy as jnp
from jax import lax
from jax.sharding import PartitionSpec as P


def tile_products(tiles, blocks, index, transpose):
    picked = jnp.take(blocks, index, axis=0)
    form = "tji,tjf->tif" if transpose else "tij,tjf->tif"
    return jnp.einsum(form, tiles, picked, preferred_element_type=jnp.float32)


def place_terms(terms, index, live, count):
    target = jnp.where(live, index, count)
    placed = jax.ops.segment_sum(terms, target, num_segments=count)
    return placed.reshape(count * terms.shape[1], terms.shape[2])


def per_device(features, weight, cotangent, tile_rows, tile_cols, tile_values, tile_count):
    rows_dev, width = features.shape
    tile = tile_values.shape[-1]
    blocks_dev = rows_dev // tile
    row_blocks = lax.axis_size("col") * blocks_dev
    col_blocks = lax.axis_size("row") * blocks_dev
    tiles = tile_values[0, 0]
    row_index = tile_rows[0, 0]
    col_index = tile_cols[0, 0]
    live = jnp.arange(tiles.shape[0], dtype=jnp.int32) < tile_count[0, 0]
    column_feats = lax.all_gather(features, "row", axis=0, tiled=True).reshape(
        col_blocks, tile, width
    )
    partial_value = place_terms(
        tile_products(tiles, column_feats, col_index, False), row_index, live, row_blocks
    )
    summed = lax.psum_scatter(partial_value, "col", scatter_dimension=0, tiled=True).astype(
        jnp.bfloat16
    )
    pre = jnp.dot(summed, weight, preferred_element_type=jnp.float32)
    sig = jax.nn.sigmoid(pre)
    hidden = (pre * sig).astype(jnp.bfloat16)
    grad_pre = (cotangent.astype(jnp.float32) * sig * (1.0 + pre * (1.0 - sig))).astype(
        jnp.bfloat16
    )
    local_weight = jnp.einsum("nf,ng->fg", summed, grad_pre, preferred_element_type=jnp.float32)
    grad_own = jnp.einsum("ng,fg->nf", grad_pre, weight, preferred_element_type=jnp.float32).astype(
        jnp.bfloat16
    )
    grad_group = lax.all_gather(grad_own, "col", axis=0, tiled=True)
    grad_weight = lax.psum(local_weight, ("row", "col"))
    grad_blocks = grad_group.reshape(row_blocks, tile, width)
    back = place_terms(
        tile_products(tiles, grad_blocks, row_index, True), col_index, live, col_blocks
    )
    grad_feat = lax.psum_scatter(back.astype(jnp.bfloat16), "row", scatter_dimension=0, tiled=True)
    return (hidden, grad_feat, grad_weight)


def solution(mesh):
    placed = (
        P(("row", "col"), None),
        P(),
        P(("row", "col"), None),
        P("row", "col", None),
        P("row", "col", None),
        P("row", "col", None, None, None),
        P("row", "col"),
    )
    return jax.shard_map(
        per_device,
        mesh=mesh,
        in_specs=placed,
        out_specs=(P(("row", "col"), None), P(("row", "col"), None), P()),
        check_vma=False,
    )
```

profile of v0, /device:TPU:1, one launch (start us, length us, event | category | flops | bytes accessed | tf_op | source)
XLA Modules:
  0.0 794.5 jit_solution(2468757312037919649)
XLA Ops:
  7.2 0.0 copy-start
  7.2 0.0 all-gather.3.cloned.1.call-start
  7.2 0.7 all-gather.3.cloned.1.call-update
  7.9 0.0 reduce-scatter.3.cloned.1.call-start
  8.6 0.7 fusion.13
  9.3 0.7 compare_and_fusion.1
  10.0 58.1 %all-gather.3.cloned.1.call-done = bf16[4096,256]{1,0:T(8,128)(2,1)} async-done(((bf16[512,256]{1,0:T(8,128)(2,1)}), bf16[4096,256]{1,0:T(8,128)(2,1)}) %all-gather.3.cloned.1.call-update) | async-done | bytes 2097168 | tf_op jit(solution)/shard_map/all_gather | solution.py:29
  68.1 8.2 %gather_fusion = bf16[128,128,256]{2,1,0:T(8,128)(2,1)} fusion(bf16[32,128,256]{2,1,0:T(8,128)(2,1)} %bitcast.38, s32[1024]{0:T(1024)S(1)} %pad_clamp_fusion.1), kind=kCustom, calls=%fused_computation | custom fusion | bytes 16777728 | tf_op jit(solution)/shard_map/jit(_take)/gather | solution.py:8
  76.3 13.2 %convolution_bitcast_fusion.1 = f32[128,128,256]{1,2,0:T(8,128)} fusion(bf16[128,128,256]{2,1,0:T(8,128)(2,1)} %gather_fusion, pred[128]{0:T(512)(128)(4,1)S(1)} %compare_and_fusion.1, bf16[1,1,128,128,128]{4,3,2,1,0:T(8,128)(2,1)} %param.12), kind=kOutput, calls=%fused_computation.5 | convolution fusion | flops 1077936128 | bytes 29360256 | tf_op jit(solution)/shard_map/tij,tjf->tif/dot_general | solution.py:10
  89.4 17.4 %copy.13 = f32[128,128,256]{2,1,0:T(8,128)} copy(f32[128,128,256]{1,2,0:T(8,128)} %convolution_bitcast_fusion.1) | data formatting | bytes 33554432 | tf_op jit(solution)/shard_map/tij,tjf->tif/dot_general | solution.py:10
  106.9 7.8 broadcast_in_dim.33
  114.7 37.7 %scatter_fusion = f32[128,128,256]{2,1,0:T(8,128)} fusion(f32[128,128,256]{2,1,0:T(8,128)} %broadcast_in_dim.33, s32[128]{0:T(128)S(1)} %get-tuple-element.9, f32[128,128,256]{2,1,0:T(8,128)} %copy.13), kind=kCustom, calls=%fused_computation.2 | custom fusion | flops 4194304 | bytes 50332160 | tf_op jit(solution)/shard_map/scatter-add | solution.py:15
  152.4 0.0 copy-start.3
  152.4 0.0 copy-start.2
  152.4 0.0 reduce-scatter.3.cloned.1.call-update
  152.5 0.0 all-gather.5.cloned.1.call-start
  152.5 215.7 %reduce-scatter.3.cloned.1.call-done = f32[512,256]{1,0:T(8,128)} async-done(((f32[16384,256]{1,0:T(8,128)}), f32[512,256]{1,0:T(8,128)}) %reduce-scatter.3.cloned.1.call-update) | async-done | bytes 524304 | tf_op jit(solution)/shard_map/reduce_scatter | solution.py:35
  368.2 0.0 copy-done
  368.2 0.0 copy-done.3
  368.2 2.2 multiply_convert_fusion
  370.4 1.0 convolution_convert_fusion
  371.4 0.0 all-gather.5.cloned.1.call-update
  371.4 0.0 all-reduce.2.cloned.1.call-start
  371.4 0.0 copy-done.2
  371.5 2.0 fusion.8
  373.5 0.0 all-reduce.2.cloned.1.call-update
  373.5 0.2 reduce-scatter.5.cloned.1.call-start
  373.7 102.7 %all-gather.5.cloned.1.call-done = bf16[16384,256]{1,0:T(8,128)(2,1)} async-done(((bf16[512,256]{1,0:T(8,128)(2,1)}), bf16[16384,256]{1,0:T(8,128)(2,1)}) %all-gather.5.cloned.1.call-update) | async-done | bytes 8388624 | tf_op jit(solution)/shard_map/all_gather | solution.py:48
  476.4 10.0 %gather_fusion.1 = bf16[128,128,256]{2,1,0:T(8,128)(2,1)} fusion(bf16[128,128,256]{2,1,0:T(8,128)(2,1)} %bitcast.39, s32[1024]{0:T(1024)S(1)} %pad_clamp_fusion), kind=kCustom, calls=%fused_computation.1 | custom fusion | bytes 16777728 | tf_op jit(solution)/shard_map/jit(_take)/gather | solution.py:8
  486.4 12.8 %convolution_bitcast_fusion = f32[128,128,256]{1,2,0:T(8,128)} fusion(bf16[128,128,256]{2,1,0:T(8,128)(2,1)} %gather_fusion.1, pred[128]{0:T(512)(128)(4,1)S(1)} %compare_and_fusion, bf16[1,1,128,128,128]{4,3,2,1,0:T(8,128)(2,1)} %param.12), kind=kOutput, calls=%fused_computation.4 | convolution fusion | flops 1077936128 | bytes 29360256 | tf_op jit(solution)/shard_map/tji,tjf->tif/dot_general | solution.py:10
  499.2 17.5 %copy.15 = f32[128,128,256]{2,1,0:T(8,128)} copy(f32[128,128,256]{1,2,0:T(8,128)} %convolution_bitcast_fusion) | data formatting | bytes 33554432 | tf_op jit(solution)/shard_map/tji,tjf->tif/dot_general | solution.py:10
  516.7 2.4 broadcast_in_dim.37
  519.1 0.0 copy-start.1
  519.1 37.2 %scatter_fusion.1 = f32[32,128,256]{2,1,0:T(8,128)} fusion(f32[32,128,256]{2,1,0:T(8,128)} %broadcast_in_dim.37, s32[128]{0:T(128)S(1)} %get-tuple-element.7, f32[128,128,256]{2,1,0:T(8,128)} %copy.15), kind=kCustom, calls=%fused_computation.3 | custom fusion | flops 4194304 | bytes 50332160 | tf_op jit(solution)/shard_map/scatter-add | solution.py:15
  556.3 3.9 convert_element_type.26
  560.2 0.0 reduce-scatter.5.cloned.1.call-update
  560.2 168.1 %all-reduce.2.cloned.1.call-done = f32[256,256]{1,0:T(8,128)} async-done(((f32[256,256]{1,0:T(8,128)}), f32[256,256]{1,0:T(8,128)}) %all-reduce.2.cloned.1.call-update) | async-done | bytes 262160 | tf_op jit(solution)/shard_map/psum | solution.py:49
  728.2 58.1 %reduce-scatter.5.cloned.1.call-done = bf16[512,256]{1,0:T(8,128)(2,1)} async-done(((bf16[4096,256]{1,0:T(8,128)(2,1)}), bf16[512,256]{1,0:T(8,128)(2,1)}) %reduce-scatter.5.cloned.1.call-update) | async-done | bytes 262160 | tf_op jit(solution)/shard_map/reduce_scatter | solution.py:54
  786.3 1.7 copy.22
  788.0 0.0 copy-done.1
  (3 shorter events, 0.0 us)
Async XLA Ops:
  7.2 361.1 %copy-start = (bf16[256,256]{1,0:T(8,128)(2,1)S(1)}, bf16[256,256]{1,0:T(8,128)(2,1)}, u32[]{:S(2)}) copy-start(bf16[256,256]{1,0:T(8,128)(2,1)} %param.8) | copy-start | bytes 393220
  7.2 60.9 %all-gather.3.cloned.1.call-start = ((), (), s32[]{:S(2)}) async-start(), calls=%async_computation.2 | async-start | bytes 2359296 | tf_op jit(solution)/shard_map/all_gather | solution.py:29
  7.9 360.3 %reduce-scatter.3.cloned.1.call-start = ((), (), s32[]{:S(2)}) async-start(), calls=%async_computation.3 | async-start | bytes 17301504 | tf_op jit(solution)/shard_map/reduce_scatter | solution.py:35
  152.4 215.8 %copy-start.3 = (bf16[512,256]{1,0:T(8,128)(2,1)S(1)}, bf16[512,256]{1,0:T(8,128)(2,1)}, u32[]{:S(2)}) copy-start(bf16[512,256]{1,0:T(8,128)(2,1)} %param.9) | copy-start | bytes 786436
  152.4 219.0 %copy-start.2 = (s32[1,1,128]{2,1,0:T(1,128)S(1)}, s32[1,1,128]{2,1,0:T(1,128)}, u32[]{:S(2)}) copy-start(s32[1,1,128]{2,1,0:T(1,128)} %param.10) | copy-start | bytes 1540
  152.5 324.0 %all-gather.5.cloned.1.call-start = ((), (), s32[]{:S(2)}) async-start(), calls=%async_computation.4 | async-start | bytes 8650752 | tf_op jit(solution)/shard_map/all_gather | solution.py:48
  371.4 356.9 %all-reduce.2.cloned.1.call-start = ((), (), s32[]{:S(2)}) async-start(), calls=%async_computation.6 | async-start | bytes 524288 | tf_op jit(solution)/shard_map/psum | solution.py:49
  373.5 412.8 %reduce-scatter.5.cloned.1.call-start = ((), (), s32[]{:S(2)}) async-start(), calls=%async_computation.5 | async-start | bytes 2359296 | tf_op jit(solution)/shard_map/reduce_scatter | solution.py:54
  519.1 268.9 %copy-start.1 = (bf16[256,256]{1,0:T(8,128)(2,1)S(1)}, bf16[256,256]{1,0:T(8,128)(2,1)}, u32[]{:S(2)}) copy-start(bf16[256,256]{1,0:T(8,128)(2,1)} %param.8) | copy-start | bytes 393220
Sparse Core Ops, SparseCore 0:
  9.8 58.2 all-gather.2
  152.6 215.6 reduce-scatter.2
  372.0 104.3 all-gather.4
  483.2 245.0 all-reduce.1
  731.4 54.9 reduce-scatter.4
where the time goes:
time: 795 us
  waiting for transfers between devices  603 us (76%)
  other arithmetic  80.1 us (10%)
  local copies, waits for them, and re-layouts  65 us (8%)
  matrix products  31.2 us (4%)
  between operations  14.5 us (2%)
    reduce_scatter x1, waiting for transfers between devices, per_device(): lax.psum_scatter(partial_value, 'col', scatter_dimension=0, tiled=True)  216 us
    psum x1, waiting for transfers between devices, per_device(): grad_weight = lax.psum(local_weight, ('row', 'col'))  168 us
    all_gather x1, waiting for transfers between devices, per_device(): grad_group = lax.all_gather(grad_own, 'col', axis=0, tiled=True)  103 us
    scatter-add x2, other arithmetic, place_terms(): placed = jax.ops.segment_sum(terms, target, num_segments=count)  74.8 us
    all_gather x1, waiting for transfers between devices, per_device(): lax.all_gather(features, 'row', axis=0, tiled=True)  58.1 us
    reduce_scatter x1, waiting for transfers between devices, per_device(): lax.psum_scatter(back.astype(jnp.bfloat16), 'row', scatter_dimension=0, t...  58.1 us
    dot_general x2, local copies, waits for them, and re-layouts, tile_products(): return jnp.einsum(form, tiles, picked, preferred_element_type=jnp.float32)  34.9 us
    dot_general x2, matrix products, tile_products(): return jnp.einsum(form, tiles, picked, preferred_element_type=jnp.float32)  26 us
  transfers between devices with their start and end apart: 5, of which 5 were waited for; matrix products, arithmetic and copies ran while one was open for 11% of the time, Pallas kernels for 0%

commit v1 on v0

v1 whole, which is shorter than its diff:
```python
import functools

import jax
import jax.numpy as jnp
from jax import lax
from jax.experimental import pallas as pl
from jax.experimental.pallas import tpu as pltpu
from jax.sharding import PartitionSpec as P

MESH = pl.DeviceIdType.MESH
BF16 = jnp.bfloat16
F32 = jnp.float32
T = 128
HALF = 128
COPIES = 340
GROUP = 8
URGENT = (4, 3, 5, 2, 6, 1, 7, 0)


def position():
    row, col = lax.axis_index("row"), lax.axis_index("col")
    return dict(
        x_hi=col // 16, z=lax.rem(col // 2, 8), core=lax.rem(col, 2), y=row // 2, x_lo=lax.rem(row, 2)
    )


def device(here, x_hi=0, x_lo=0, y=0, z=0, core=0):
    x_hi = 1 - here["x_hi"] if x_hi else here["x_hi"]
    x_lo = 1 - here["x_lo"] if x_lo else here["x_lo"]
    core = 1 - here["core"] if core else here["core"]
    y = lax.rem(here["y"] + y, 4)
    z = lax.rem(here["z"] + z, 8)
    return (y * 2 + x_lo, x_hi * 16 + z * 2 + core)


ROW_TILE, ROW_FEAT, ROW_KEEP, ROW_LAST, COL_TILE, COL_GRAD, COL_KEEP, COL_LAST = range(8)


def order_kernel(count_ref, rows_ref, cols_ref, table_ref):
    here = position()
    lane = lax.broadcasted_iota(jnp.int32, (T, T), 1)
    sub = lax.broadcasted_iota(jnp.int32, (T, T), 0)
    eye = lane == sub
    count = count_ref[0, 0]

    def spread(values):
        return jnp.broadcast_to(values, (T, T))

    def column(values):
        kept = jnp.where(eye, spread(values), 0).astype(F32)
        return jnp.broadcast_to(jnp.sum(kept, axis=1, keepdims=True), (T, T)).astype(jnp.int32)

    def total(values):
        return jnp.sum(values.astype(F32), axis=0, keepdims=True).astype(jnp.int32)

    live_down = sub < count

    def feat_place(cols):
        owner = cols // 4
        return ((lax.rem(owner, 2) + here["x_lo"]) % 2 * 4 + (owner // 2 - here["y"] + 4) % 4) * 4 + lax.rem(cols, 4)

    def grad_place(rows):
        owner, block = rows // 4, lax.rem(rows, 4)
        x_other = (owner // 16 + here["x_hi"]) % 2
        z_away = (lax.rem(owner // 2, 8) - here["z"] + 8) % 8
        core_other = (lax.rem(owner, 2) + here["core"]) % 2
        place = jnp.where(block < 2, 2 * block + x_other, 2 + block + 2 * x_other)
        return (core_other * 8 + z_away) * 8 + place

    rows, cols = rows_ref[...], cols_ref[...]
    rows_down, cols_down = grad_place(column(rows)), feat_place(column(cols))
    rows, cols = grad_place(rows), feat_place(cols)

    def sorted_by(keys, keys_down, value_down):
        big = T * T
        key = jnp.where(lane < count, spread(keys) * T + lane, big + lane)
        key_down = jnp.where(live_down, keys_down * T + sub, big + sub)
        rank_down = jnp.sum((key < key_down).astype(F32), axis=1, keepdims=True)
        rank_down = jnp.broadcast_to(rank_down, (T, T)).astype(jnp.int32)
        now = rank_down == lane
        tile = total(jnp.where(now, sub, 0))
        value = total(jnp.where(now, value_down, 0))
        mine = total(jnp.where(now, keys_down, 0))
        before = total(jnp.where(rank_down == lane - 1, keys_down, 0))
        first = lax.broadcasted_iota(jnp.int32, (1, T), 1) == 0
        keep = jnp.where(jnp.logical_or(first, mine != before), 0, 1)
        upto = total(jnp.where(jnp.logical_and(live_down, keys_down <= lane), 1, 0))
        some = total(jnp.where(jnp.logical_and(live_down, keys_down == lane), 1, 0))
        return [tile, value, keep, jnp.where(some > 0, upto - 1, T)]

    lines = sorted_by(rows, rows_down, cols_down) + sorted_by(cols, cols_down, rows_down)
    for number, line in enumerate(lines):
        table_ref[number : number + 1, :] = line


def each(count, body):
    def step(i, carried):
        body(i)
        return carried

    lax.fori_loop(0, count, step, 0)


def add_up(out, terms):
    def body(i):
        rows = pl.ds(i * 32, 32)
        total = terms[0][:, rows].astype(F32)
        for term in terms[1:]:
            total = total + term[:, rows].astype(F32)
        out[:, rows] = total.astype(out.dtype)

    each(T // 32, body)


class Links:
    def __init__(self, send_sem, recv_sem):
        self.send_sem, self.recv_sem, self.copies = send_sem, recv_sem, []

    def send(self, src, dst, to):
        number = len(self.copies)
        copy = pltpu.make_async_remote_copy(
            src_ref=src,
            dst_ref=dst,
            send_sem=self.send_sem.at[number],
            recv_sem=self.recv_sem.at[number],
            device_id=to,
            device_id_type=MESH,
        )
        copy.start()
        self.copies.append(copy)
        return copy


def layer_kernel(
    table,
    feat_hbm,
    weight,
    cot_hbm,
    tile_hbm,
    hidden,
    grad_feat,
    grad_weight,
    tiles,
    cot,
    feats0,
    feats1,
    slots,
    give,
    core_in,
    value,
    x_in,
    ring_in,
    x_last,
    part,
    summed,
    grads0,
    grads1,
    carry,
    back,
    back_x,
    back_y,
    back_y2,
    back_x2,
    w_sum,
    w_own,
    w_core,
    w_y,
    w_z,
    w_x,
    w_all_z,
    w_all_y,
    w_all,
    local_sem,
    send_sem,
    recv_sem,
):
    here = position()
    feats, grads = (feats0, feats1), (grads0, grads1)
    links = Links(send_sem, recv_sem)
    z_up, z_down = device(here, z=1), device(here, z=7)
    x_far, x_near = device(here, x_hi=1), device(here, x_lo=1)
    x_both = device(here, x_hi=1, x_lo=1)
    twin = device(here, core=1)
    y_to = {d: device(here, y=d) for d in (1, 2, 3)}
    z_to = {d: device(here, z=d) for d in range(1, 8)}

    loads = [
        pltpu.make_async_copy(feat_hbm.at[:, :, pl.ds(f * HALF, HALF)], feats[f].at[pl.ds(0, 4)], local_sem.at[f])
        for f in range(2)
    ]
    loads.append(pltpu.make_async_copy(tile_hbm, tiles, local_sem.at[2]))
    loads.append(pltpu.make_async_copy(cot_hbm, cot, local_sem.at[3]))
    for load in loads:
        load.start()

    barrier = pltpu.get_barrier_semaphore()
    partners = [x_far, x_near, x_both, twin, *y_to.values(), *z_to.values()]
    for partner in partners:
        pl.semaphore_signal(barrier, inc=1, device_id=partner, device_id_type=MESH)
    for f in range(2):
        slots[f, T] = jnp.zeros((T, HALF), BF16)
    loads[0].wait()
    loads[1].wait()
    pl.semaphore_wait(barrier, len(partners))

    def gather_first(f):
        own = feats[f].at[pl.ds(0, 4)]
        near = links.send(own, feats[f].at[pl.ds(16, 4)], x_near)
        over = {d: links.send(own, feats[f].at[pl.ds((4 - d) * 4, 4)], y_to[d]) for d in (1, 3, 2)}
        return near, over

    def gather_second(f, first):
        near, over = first
        near.wait_recv()
        copies = [
            links.send(feats[f].at[pl.ds(16, 2)], feats[f].at[pl.ds(16 + (4 - d) * 4, 2)], y_to[d])
            for d in (1, 3, 2)
        ]
        for d in (1, 3, 2):
            over[d].wait_recv()
            rows = (4 - d) * 4 + 2
            copies.append(links.send(feats[f].at[pl.ds(rows, 2)], feats[f].at[pl.ds(16 + rows, 2)], x_near))
        return copies

    def products(f, piece, pieces, back_pass):
        tile_line, value_line, keep_line = (
            (COL_TILE, COL_GRAD, COL_KEEP) if back_pass else (ROW_TILE, ROW_FEAT, ROW_KEEP)
        )
        steps = T // GROUP // pieces
        source = (grads if back_pass else feats)[f]

        def step(i):
            total = carry[...]
            for u in range(GROUP):
                t = i * GROUP + u
                tile = tiles[table[tile_line, t]]
                block = source[table[value_line, t]]
                if back_pass:
                    tile = tile.T
                term = jnp.dot(tile, block, preferred_element_type=F32)
                total = term + total * table[keep_line, t].astype(F32)
                slots[f, t] = total.astype(BF16)
            carry[...] = total

        each(steps, lambda i: step(piece * steps + i))

    def core_send(f):
        copies = {}
        for dz in URGENT:

            def fill(place, dz=dz):
                give[f, dz * 8 + place] = slots[f, table[ROW_LAST, 64 + dz * 8 + place]]

            each(8, fill)
            span = pl.ds(dz * 8, 8)
            copies[dz] = links.send(give.at[f, span], core_in.at[f, span], twin)
        return copies

    def core_sum(f, dz, copies):
        copies[dz].wait_recv()

        def fill(place):
            at = dz * 8 + place
            own = slots[f, table[ROW_LAST, at]].astype(F32)
            value[f, at] = (own + core_in[f, at].astype(F32)).astype(BF16)

        each(8, fill)
        return links.send(value.at[f, pl.ds(dz * 8 + 6, 2)], x_in.at[f, pl.ds(dz * 2, 2)], x_far)

    class Ring:
        def __init__(self, f, stream, x_copies=None):
            self.f, self.stream, self.x_copies = f, stream, x_copies
            self.up = self.down = None

        def span(self, dz, first=0, size=2):
            return value.at[self.f, pl.ds(dz * 8 + self.stream * 2 + first, size)]

        def own(self, dz, first=0, size=2):
            if self.x_copies is None:
                return [self.span(dz, first, size)]
            return [self.span(dz, first, size), x_in.at[self.f, pl.ds(dz * 2 + first, size)]]

        def slot(self, way, step, first=0, size=2):
            return ring_in.at[self.f, self.stream, way, pl.ds(step * 2 + first, size)]

        def step(self, s):
            if s == 0:
                if self.x_copies is not None:
                    self.x_copies[4].wait_recv()
                    add_up(self.span(4), self.own(4))
                self.up = links.send(self.span(4, 0, 1), self.slot(0, 0, 0, 1), z_up)
                self.down = links.send(self.span(4, 1, 1), self.slot(1, 0, 1, 1), z_down)
                return
            for way, dz in ((0, 4 - s), (1, 4 + s)):
                if self.x_copies is not None:
                    self.x_copies[dz].wait_recv()
                (self.up, self.down)[way].wait_recv()
                if s == 1:
                    add_up(self.span(dz, way, 1), self.own(dz, way, 1) + [self.slot(way, 0, way, 1)])
                    if self.x_copies is not None:
                        add_up(self.span(dz, 1 - way, 1), self.own(dz, 1 - way, 1))
                else:
                    add_up(self.span(dz), self.own(dz) + [self.slot(way, s - 1)])
                sent = links.send(self.span(dz), self.slot(way, s), (z_up, z_down)[way])
                if way == 0:
                    self.up = sent
                else:
                    self.down = sent

        def finish(self):
            if self.x_copies is not None:
                self.x_copies[0].wait_recv()
            self.up.wait_recv()
            self.down.wait_recv()

        def last(self, first, size):
            return self.own(0, first, size) + [self.slot(0, 3, first, size), self.slot(1, 3, first, size)]

    def finish_z(f, b, ring):
        ring.finish()
        far = pl.ds(2 * f + b, 1)
        add_up(x_last.at[0, far], ring.last(1, 1))
        copy = links.send(x_last.at[0, far], x_last.at[1, far], x_far)
        add_up(part.at[f, pl.ds(b, 1)], ring.last(0, 1))
        return copy

    def close_z(f, b, copy):
        copy.wait_recv()
        add_up(
            summed.at[pl.ds(b, 1), :, pl.ds(f * HALF, HALF)],
            [part.at[f, pl.ds(b, 1)], x_last.at[1, pl.ds(2 * f + b, 1)]],
        )

    def close_x(f, ring):
        ring.finish()
        add_up(summed.at[pl.ds(2, 2), :, pl.ds(f * HALF, HALF)], ring.last(0, 2))

    def middle(pair):
        def body(i):
            b = 2 * pair + i
            rows = summed[b]
            pre = jnp.dot(rows, weight[...], preferred_element_type=F32)
            sig = jax.nn.sigmoid(pre)
            hidden[b] = (pre * sig).astype(BF16)
            grad_pre = (cot[b].astype(F32) * sig * (1.0 + pre * (1.0 - sig))).astype(BF16)
            own = lax.dot_general(
                grad_pre, weight[...], (((1,), (1,)), ((), ())), preferred_element_type=F32
            )
            place = 2 * i if pair == 0 else 4 + i
            for f in range(2):
                grads[f][place] = own[:, f * HALF : (f + 1) * HALF].astype(BF16)
            w_sum[...] += jnp.dot(rows.T, grad_pre, preferred_element_type=F32)

        each(2, body)

    first = gather_first(0)
    second = gather_second(0, first)
    first1 = gather_first(1)
    loads[2].wait()
    loads[3].wait()
    w_sum[...] = jnp.zeros_like(w_sum)
    carry[...] = jnp.zeros_like(carry)
    for copy in second:
        copy.wait_recv()
    products(0, 0, 1, False)
    core0 = core_send(0)
    second1 = gather_second(1, first1)
    x0 = {}
    z0 = [Ring(0, 0), Ring(0, 1)]
    for dz in URGENT:
        x0[dz] = core_sum(0, dz, core0)
        if dz == 4:
            for ring in z0:
                ring.step(0)
    for ring in z0:
        ring.step(1)
    for copy in second1:
        copy.wait_recv()
    for piece in range(2):
        products(1, piece, 2, False)
        for ring in z0:
            ring.step(2 + piece)
    core1 = core_send(1)
    last = {}
    for b in range(2):
        last[0, b] = finish_z(0, b, z0[b])
    x1 = {}
    ring_x0 = Ring(0, 2, x0)
    z1 = [Ring(1, 0), Ring(1, 1)]
    ring_x0.step(0)
    for dz in URGENT:
        x1[dz] = core_sum(1, dz, core1)
        if dz == 4:
            for ring in z1:
                ring.step(0)
    for s in range(1, 4):
        ring_x0.step(s)
        for ring in z1:
            ring.step(s)
    ring_x1 = Ring(1, 2, x1)
    ring_x1.step(0)
    close_x(0, ring_x0)
    for b in range(2):
        last[1, b] = finish_z(1, b, z1[b])
    ring_x1.step(1)
    for b in range(2):
        for f in range(2):
            close_z(f, b, last[f, b])
    ring_x1.step(2)
    ring_x1.step(3)
    middle(0)

    def spread_near(f, b):
        return links.send(grads[f].at[pl.ds(2 * b, 1)], grads[f].at[pl.ds(2 * b + 1, 1)], x_far)

    class Spread:
        def __init__(self, f, stream):
            self.f, self.stream = f, stream
            self.up = self.down = None

        def span(self, dz, first=0, size=2):
            return self.at(self.f, dz, self.stream * 2 + first, size)

        @staticmethod
        def at(f, dz, place, size):
            return grads[f].at[pl.ds((dz % 8) * 8 + place, size)]

        def step(self, s):
            if s > 0:
                self.up.wait_recv()
                self.down.wait_recv()
            first, size = ((0, 2), (1, 1))[s == 3]
            self.up = links.send(
                self.span(-s, 0, size), self.span(-s - 1, 0, size), z_up
            )
            self.down = links.send(self.span(s, first, size), self.span(s + 1, first, size), z_down)

        def done(self):
            self.up.wait_recv()
            self.down.wait_recv()

    def to_twin(f, dz, place, size):
        at = (dz % 8) * 8 + place
        return links.send(grads[f].at[pl.ds(at, size)], grads[f].at[pl.ds(64 + at, size)], twin)

    def to_far(f, dz):
        at = (dz % 8) * 8
        return links.send(grads[f].at[pl.ds(at + 4, 2)], grads[f].at[pl.ds(at + 6, 2)], x_far)

    near = {(f, b): spread_near(f, b) for f in range(2) for b in range(2)}
    close_x(1, ring_x1)
    middle(1)
    streams = {f: [Spread(f, 0), Spread(f, 1), Spread(f, 2)] for f in range(2)}
    from_far = {0: {}, 1: {}}
    from_twin = {0: [], 1: []}

    def round_of(f, s):
        for k in (2, 0, 1):
            if s == 0 and k < 2:
                near[f, k].wait_recv()
            if s < 4:
                streams[f][k].step(s)
            else:
                streams[f][k].done()
            if k == 2:
                for dz in sorted({-s % 8, s % 8}):
                    from_far[f][dz] = to_far(f, dz)
                    from_twin[f].append(to_twin(f, dz, 4, 2))
        for dz in sorted({-s % 8, s % 8}):
            from_twin[f].append(to_twin(f, dz, 0, 4))

    def far_to_twin(f, dzs):
        for dz in dzs:
            from_far[f][dz % 8].wait_recv()
            from_twin[f].append(to_twin(f, dz, 6, 2))

    def all_here(f):
        for copy in from_twin[f]:
            copy.wait_recv()

    def weight_start():
        def fill(i):
            for j in range(2):
                w_own[2 * i + j] = w_sum[pl.ds(8 * i, 8), j * 128 : (j + 1) * 128]

        each(32, fill)
        return links.send(w_own.at[pl.ds((1 - here["core"]) * 32, 32)], w_core.at[0], twin)

    def weight_y(copy):
        copy.wait_recv()

        def fill(i):
            w_core[1, i] = w_own[here["core"] * 32 + i] + w_core[0, i]

        each(32, fill)
        return [
            links.send(w_core.at[1, pl.ds(lax.rem(here["y"] + d, 4) * 8, 8)], w_y.at[d], y_to[d]) for d in (1, 2, 3)
        ]

    def weight_z(copies):
        for copy in copies:
            copy.wait_recv()

        def fill(i):
            w_y[0, i] = w_core[1, here["y"] * 8 + i] + w_y[1, i] + w_y[2, i] + w_y[3, i]

        each(8, fill)
        return [
            links.send(w_y.at[0, pl.ds(lax.rem(here["z"] + d, 8), 1)], w_z.at[pl.ds(d, 1)], z_to[d])
            for d in range(1, 8)
        ]

    def weight_x(copies):
        for copy in copies:
            copy.wait_recv()
        total = w_y[0, pl.ds(here["z"], 1)]
        for d in range(1, 8):
            total = total + w_z[d : d + 1]
        w_x[0:1] = total
        return [
            links.send(w_x.at[pl.ds(0, 1)], w_x.at[pl.ds(i, 1)], to)
            for i, to in ((1, x_far), (2, x_near), (3, x_both))
        ]

    def weight_all_z(copies):
        for copy in copies:
            copy.wait_recv()
        mine = pl.ds(here["z"], 1)
        w_all_z[mine] = (w_x[0:1] + w_x[1:2]) + (w_x[2:3] + w_x[3:4])
        return [links.send(w_all_z.at[mine], w_all_z.at[mine], z_to[d]) for d in range(1, 8)]

    def weight_all_y(copies):
        for copy in copies:
            copy.wait_recv()
        mine = pl.ds(here["y"] * 8, 8)

        def fill(i):
            w_all_y[here["y"] * 8 + i] = w_all_z[i]

        each(8, fill)
        return [links.send(w_all_y.at[mine], w_all_y.at[mine], y_to[d]) for d in (1, 2, 3)]

    def weight_all_core(copies):
        for copy in copies:
            copy.wait_recv()
        mine = pl.ds(here["core"] * 32, 32)

        def fill(i):
            w_all[here["core"] * 32 + i] = w_all_y[i]

        each(32, fill)
        return links.send(w_all.at[mine], w_all.at[mine], twin)

    def weight_end(copy):
        copy.wait_recv()

        def fill(i):
            for j in range(2):
                grad_weight[pl.ds(8 * i, 8), j * 128 : (j + 1) * 128] = w_all[2 * i + j]

        each(32, fill)

    def back_first(f):
        def fill(place):
            back[f, place] = slots[f, table[COL_LAST, place]]

        each(32, fill)
        near_copies = {
            d: links.send(back.at[f, pl.ds((4 + d) * 4, 2)], back_x.at[f, pl.ds(d * 2, 2)], x_near)
            for d in (2, 1, 3, 0)
        }
        y_copies = [
            links.send(back.at[f, pl.ds((x_other * 4 + d) * 4 + 2, 2)], back_y.at[f, d, pl.ds(x_other * 2, 2)], y_to[d])
            for x_other in (1, 0)
            for d in (2, 1, 3)
        ]
        return near_copies, y_copies

    def back_second(f, first):
        near_copies, y_copies = first
        y_second = []
        for d in (2, 1, 3, 0):
            near_copies[d].wait_recv()
            own = back.at[f, pl.ds(d * 4, 2)]
            add_up(own, [own, back_x.at[f, pl.ds(d * 2, 2)]])
            if d:
                y_second.append(links.send(back.at[f, pl.ds(d * 4, 2)], back_y2.at[f, d], y_to[d]))
        for copy in y_copies[:3]:
            copy.wait_recv()
        add_up(
            back_x2.at[f, pl.ds(0, 2)],
            [back.at[f, pl.ds(18, 2)]] + [back_y.at[f, d, pl.ds(2, 2)] for d in (1, 2, 3)],
        )
        near_second = links.send(back_x2.at[f, pl.ds(0, 2)], back_x2.at[f, pl.ds(2, 2)], x_near)
        return y_copies[3:], y_second, near_second

    def back_third(f, second):
        y_copies, y_second, near_second = second
        lanes = pl.ds(f * HALF, HALF)
        for copy in y_copies + [near_second]:
            copy.wait_recv()
        add_up(
            grad_feat.at[pl.ds(2, 2), :, lanes],
            [back.at[f, pl.ds(2, 2)], back_x2.at[f, pl.ds(2, 2)]]
            + [back_y.at[f, d, pl.ds(0, 2)] for d in (1, 2, 3)],
        )
        for copy in y_second:
            copy.wait_recv()
        add_up(
            grad_feat.at[pl.ds(0, 2), :, lanes],
            [back.at[f, pl.ds(0, 2)]] + [back_y2.at[f, d] for d in (1, 2, 3)],
        )

    round_of(0, 0)
    w_copy = weight_start()
    round_of(0, 1)
    w_copy = weight_y(w_copy)
    round_of(0, 2)
    far_to_twin(0, (0,))
    round_of(0, 3)
    w_copy = weight_z(w_copy)
    round_of(1, 0)
    far_to_twin(0, (1, 7))
    round_of(0, 4)
    round_of(1, 1)
    w_copy = weight_x(w_copy)
    far_to_twin(0, (2, 6))
    round_of(1, 2)
    far_to_twin(0, (3, 5, 4))
    w_copy = weight_all_z(w_copy)
    all_here(0)
    products(0, 0, 2, True)
    round_of(1, 3)
    products(0, 1, 2, True)
    w_copy = weight_all_y(w_copy)
    first0 = back_first(0)
    round_of(1, 4)
    far_to_twin(1, (0, 1, 7, 2, 6))
    second0 = back_second(0, first0)
    w_copy = weight_all_core(w_copy)
    far_to_twin(1, (3, 5, 4))
    all_here(1)
    products(1, 0, 1, True)
    first1 = back_first(1)
    weight_end(w_copy)
    back_third(0, second0)
    back_third(1, back_second(1, first1))
    for copy in links.copies:
        copy.wait_send()


def per_device(features, weight, cotangent, tile_rows, tile_cols, tile_values, tile_count):
    table = pl.pallas_call(
        order_kernel,
        out_shape=jax.ShapeDtypeStruct((8, T), jnp.int32),
        in_specs=[
            pl.BlockSpec(memory_space=pltpu.SMEM),
            pl.BlockSpec(memory_space=pltpu.VMEM),
            pl.BlockSpec(memory_space=pltpu.VMEM),
        ],
        out_specs=pl.BlockSpec(memory_space=pltpu.VMEM),
        name="order",
    )(tile_count, tile_rows.reshape(1, T), tile_cols.reshape(1, T))
    hbm, vmem = pl.BlockSpec(memory_space=pl.ANY), pl.BlockSpec(memory_space=pltpu.VMEM)

    def blocks(*counts):
        return pltpu.VMEM((*counts, T, HALF), BF16)

    def pieces(*counts):
        return pltpu.VMEM((*counts, 8, 128), F32)

    hidden, grad_feat, grad_weight = pl.pallas_call(
        layer_kernel,
        out_shape=(
            jax.ShapeDtypeStruct((4, T, 256), BF16),
            jax.ShapeDtypeStruct((4, T, 256), BF16),
            jax.ShapeDtypeStruct((256, 256), F32),
        ),
        in_specs=[pl.BlockSpec(memory_space=pltpu.SMEM), hbm, vmem, hbm, hbm],
        out_specs=(vmem, vmem, vmem),
        scratch_shapes=[
            blocks(T),
            pltpu.VMEM((4, T, 256), BF16),
            blocks(32),
            blocks(32),
            blocks(2, T + 1),
            blocks(2, 64),
            blocks(2, 64),
            blocks(2, 64),
            blocks(2, 16),
            blocks(2, 3, 2, 8),
            blocks(2, 4),
            pltpu.VMEM((2, 2, T, HALF), F32),
            pltpu.VMEM((4, T, 256), BF16),
            blocks(128),
            blocks(128),
            pltpu.VMEM((T, HALF), F32),
            blocks(2, 32),
            blocks(2, 8),
            blocks(2, 4, 4),
            blocks(2, 4, 2),
            blocks(2, 4),
            pltpu.VMEM((256, 256), F32),
            pieces(64),
            pieces(2, 32),
            pieces(4, 8),
            pieces(8),
            pieces(4),
            pieces(8),
            pieces(32),
            pieces(64),
            pltpu.SemaphoreType.DMA((4,)),
            pltpu.SemaphoreType.DMA((COPIES,)),
            pltpu.SemaphoreType.DMA((COPIES,)),
        ],
        compiler_params=pltpu.CompilerParams(
            collective_id=0, has_side_effects=True, vmem_limit_bytes=60 * 2**20
        ),
        cost_estimate=pl.CostEstimate(flops=5 * 10**9, bytes_accessed=6 * 2**20, transcendentals=2**17),
        name="layer",
    )(
        table,
        features.reshape(4, T, 256),
        weight,
        cotangent.reshape(4, T, 256),
        tile_values.reshape(T, T, T),
    )
    return hidden.reshape(4 * T, 256), grad_feat.reshape(4 * T, 256), grad_weight


def solution(mesh):
    placed = (
        P(("row", "col"), None),
        P(),
        P(("row", "col"), None),
        P("row", "col", None),
        P("row", "col", None),
        P("row", "col", None, None, None),
        P("row", "col"),
    )
    return jax.shard_map(
        per_device,
        mesh=mesh,
        in_specs=placed,
        out_specs=(P(("row", "col"), None), P(("row", "col"), None), P()),
        check_vma=False,
    )
```

time: 795 us -> 153 us (0.19)
  waiting for transfers between devices: 603 us -> 0 us
  Pallas kernels: 0 us -> 146 us
  other arithmetic: 80.1 us -> 0 us
  local copies, waits for them, and re-layouts: 65 us -> 5.01 us
  matrix products: 31.2 us -> 0 us
  between operations: 14.5 us -> 1.29 us
    reduce_scatter x2 -> x0, waiting for transfers between devices: 274 us -> none  [the longest x1 216 us: per_device(): lax.psum_scatter(partial_value, 'col', scatter_dimension=0, tiled=True)]
    psum x1 -> x0, waiting for transfers between devices: 168 us -> none  [per_device(): grad_weight = lax.psum(local_weight, ('row', 'col'))]
    all_gather x2 -> x0, waiting for transfers between devices: 161 us -> none  [the longest x1 103 us: per_device(): grad_group = lax.all_gather(grad_own, 'col', axis=0, tiled=True)]
    pallas_call x0 -> x2, Pallas kernels: none -> 146 us  [the longest x1 145 us: per_device(): pl.pallas_call(layer_kernel, out_shape=(jax.ShapeDtypeStruct((4, T, 256),...]
    scatter-add x2 -> x0, other arithmetic: 74.8 us -> none  [place_terms(): placed = jax.ops.segment_sum(terms, target, num_segments=count)]
    dot_general x2 -> x0, local copies, waits for them, and re-layouts: 34.9 us -> none  [tile_products(): return jnp.einsum(form, tiles, picked, preferred_element_type=jnp.float32)]
    dot_general x5 -> x0, matrix products: 31.2 us -> none  [the longest x2 26 us: tile_products(): return jnp.einsum(form, tiles, picked, preferred_element_type=jnp.float32)]
    gather x2 -> x0, local copies, waits for them, and re-layouts: 18.1 us -> none  [tile_products(): picked = jnp.take(blocks, index, axis=0)]
  transfers between devices with their start and end apart: 5 -> 0, of which waited for: 5 -> 0; matrix products, arithmetic and copies ran while one was open for 11% -> 0% of each run, Pallas kernels for 0% -> 0%
where the time goes in v1:
time: 153 us
  Pallas kernels  146 us (95%)
  local copies, waits for them, and re-layouts  5.01 us (3%)
    pallas_call x1, Pallas kernels, per_device(): pl.pallas_call(layer_kernel, out_shape=(jax.ShapeDtypeStruct((4, T, 256),...  145 us
    unnamed x3, local copies, waits for them, and re-layouts  5.01 us

profile of v1, /device:TPU:1, one launch (start us, length us, event | category | flops | bytes accessed | tf_op | source)
XLA Modules:
  0.0 152.7 jit_solution(13743164583074937660)
XLA Ops:
  1.3 1.9 %order.1.table = s32[8,128]{1,0:T(8,128)} custom-call(s32[1,1]{1,0:T(1,128)S(6)} %copy.13.count_ref, s32[1,128]{1,0:T(1,128)} %bitcast.9, s32[1,128]{1,0:T(1,128)} %bitcast.10), custom_call_target="tpu_custom_call" | custom-call | tf_op jit(solution)/shard_map/order/pallas_call | solution.py:653
  3.2 144.6 %layer.1 = (bf16[4,128,256]{2,1,0:T(8,128)(2,1)}, bf16[4,128,256]{2,1,0:T(8,128)(2,1)}, f32[256,256]{1,0:T(8,128)}) custom-call(s32[8,128]{1,0:T(8,128)} %order.1.table, bf16[4,128,256]{2,1,0:T(8,128)(2,1)} %bitcast.12, bf16[256,256]{1,0:T(8,128)(2,1)} %weight.1, bf16[4,128,256]{2,1,0:T(8,128)(2,1)} %bitcast.13, bf16[128,128,128]{2,1,0:T(8,128)(2,1)} %bitcast.11), custom_call_target="tpu_custom_call" | custom-call | flops 5000000000 | bytes 6291456 | tf_op jit(solution)/shard_map/layer/pallas_call | solution.py:672
  147.7 1.7 %copy.14 = bf16[512,256]{1,0:T(8,128)(2,1)} copy(bf16[512,256]{1,0:T(8,128)(2,1)} %bitcast.8) | data formatting | bytes 524288
  149.4 1.7 %copy.15 = bf16[512,256]{1,0:T(8,128)(2,1)} copy(bf16[512,256]{1,0:T(8,128)(2,1)} %bitcast.7) | data formatting | bytes 524288
  151.1 1.7 %copy.16 = f32[256,256]{1,0:T(8,128)} copy(f32[256,256]{1,0:T(8,128)} %get-tuple-element.14) | data formatting | bytes 524288

commit v2 on v1

--- a/solution.py
+++ b/solution.py
@@ -33,7 +33,8 @@
     return (y * 2 + x_lo, x_hi * 16 + z * 2 + core)
 
 
-ROW_TILE, ROW_FEAT, ROW_KEEP, ROW_LAST, COL_TILE, COL_GRAD, COL_KEEP, COL_LAST = range(8)
+ROW_TILE, ROW_KEEP, ROW_LAST, ROW_FEAT, COL_TILE, COL_KEEP, COL_LAST, COL_GRAD = range(8)
+LINES = 9
 
 
 def order_kernel(count_ref, rows_ref, cols_ref, table_ref):
@@ -59,19 +60,29 @@
         owner = cols // 4
         return ((lax.rem(owner, 2) + here["x_lo"]) % 2 * 4 + (owner // 2 - here["y"] + 4) % 4) * 4 + lax.rem(cols, 4)
 
-    def grad_place(rows):
+    def row_place(rows, order):
         owner, block = rows // 4, lax.rem(rows, 4)
         x_other = (owner // 16 + here["x_hi"]) % 2
         z_away = (lax.rem(owner // 2, 8) - here["z"] + 8) % 8
         core_other = (lax.rem(owner, 2) + here["core"]) % 2
-        place = jnp.where(block < 2, 2 * block + x_other, 2 + block + 2 * x_other)
-        return (core_other * 8 + z_away) * 8 + place
+        return (core_other * 8 + z_away) * 8 + order(block, x_other)
+
+    def sum_order(block, x_other):
+        return jnp.where(block < 2, 2 * block + x_other, 2 + block + 2 * x_other)
+
+    def far_last(block, x_other):
+        return block + 4 * x_other
+
+    def far_first(block, x_other):
+        return 2 * block + x_other
 
     rows, cols = rows_ref[...], cols_ref[...]
-    rows_down, cols_down = grad_place(column(rows)), feat_place(column(cols))
-    rows, cols = grad_place(rows), feat_place(cols)
-
-    def sorted_by(keys, keys_down, value_down):
+    rows_down, cols_down = column(rows), feat_place(column(cols))
+    grads_down = [row_place(rows_down, far_last), row_place(rows_down, far_first)]
+    rows_down = row_place(rows_down, sum_order)
+    rows, cols = row_place(rows, sum_order), feat_place(cols)
+
+    def sorted_by(keys, keys_down, values_down):
         big = T * T
         key = jnp.where(lane < count, spread(keys) * T + lane, big + lane)
         key_down = jnp.where(live_down, keys_down * T + sub, big + sub)
@@ -79,16 +90,16 @@
         rank_down = jnp.broadcast_to(rank_down, (T, T)).astype(jnp.int32)
         now = rank_down == lane
         tile = total(jnp.where(now, sub, 0))
-        value = total(jnp.where(now, value_down, 0))
+        values = [total(jnp.where(now, value, 0)) for value in values_down]
         mine = total(jnp.where(now, keys_down, 0))
         before = total(jnp.where(rank_down == lane - 1, keys_down, 0))
         first = lax.broadcasted_iota(jnp.int32, (1, T), 1) == 0
         keep = jnp.where(jnp.logical_or(first, mine != before), 0, 1)
         upto = total(jnp.where(jnp.logical_and(live_down, keys_down <= lane), 1, 0))
         some = total(jnp.where(jnp.logical_and(live_down, keys_down == lane), 1, 0))
-        return [tile, value, keep, jnp.where(some > 0, upto - 1, T)]
-
-    lines = sorted_by(rows, rows_down, cols_down) + sorted_by(cols, cols_down, rows_down)
+        return [tile, keep, jnp.where(some > 0, upto - 1, T), *values]
+
+    lines = sorted_by(rows, rows_down, [cols_down]) + sorted_by(cols, cols_down, grads_down)
     for number, line in enumerate(lines):
         table_ref[number : number + 1, :] = line
 
@@ -224,7 +235,7 @@
 
     def products(f, piece, pieces, back_pass):
         tile_line, value_line, keep_line = (
-            (COL_TILE, COL_GRAD, COL_KEEP) if back_pass else (ROW_TILE, ROW_FEAT, ROW_KEEP)
+            (COL_TILE, COL_GRAD + f, COL_KEEP) if back_pass else (ROW_TILE, ROW_FEAT, ROW_KEEP)
         )
         steps = T // GROUP // pieces
         source = (grads if back_pass else feats)[f]
@@ -346,9 +357,8 @@
             own = lax.dot_general(
                 grad_pre, weight[...], (((1,), (1,)), ((), ())), preferred_element_type=F32
             )
-            place = 2 * i if pair == 0 else 4 + i
-            for f in range(2):
-                grads[f][place] = own[:, f * HALF : (f + 1) * HALF].astype(BF16)
+            grads[0][b] = own[:, :HALF].astype(BF16)
+            grads[1][2 * b] = own[:, HALF:].astype(BF16)
             w_sum[...] += jnp.dot(rows.T, grad_pre, preferred_element_type=F32)
 
         each(2, body)
@@ -365,118 +375,134 @@
     products(0, 0, 1, False)
     core0 = core_send(0)
     second1 = gather_second(1, first1)
-    x0 = {}
+    x0, x1, last = {}, {}, {}
     z0 = [Ring(0, 0), Ring(0, 1)]
+    z1 = [Ring(1, 0), Ring(1, 1)]
+    ring_x0, ring_x1 = Ring(0, 2, x0), Ring(1, 2, x1)
+
+    def step_all(rings, s):
+        for ring in rings:
+            ring.step(s)
+
     for dz in URGENT:
         x0[dz] = core_sum(0, dz, core0)
         if dz == 4:
-            for ring in z0:
-                ring.step(0)
-    for ring in z0:
-        ring.step(1)
+            step_all(z0, 0)
+    step_all(z0, 1)
+    ring_x0.step(0)
     for copy in second1:
         copy.wait_recv()
-    for piece in range(2):
-        products(1, piece, 2, False)
-        for ring in z0:
-            ring.step(2 + piece)
+    products(1, 0, 2, False)
+    step_all(z0, 2)
+    products(1, 1, 2, False)
     core1 = core_send(1)
-    last = {}
-    for b in range(2):
-        last[0, b] = finish_z(0, b, z0[b])
-    x1 = {}
-    ring_x0 = Ring(0, 2, x0)
-    z1 = [Ring(1, 0), Ring(1, 1)]
-    ring_x0.step(0)
+    step_all(z0, 3)
+    ring_x0.step(1)
     for dz in URGENT:
         x1[dz] = core_sum(1, dz, core1)
         if dz == 4:
-            for ring in z1:
-                ring.step(0)
-    for s in range(1, 4):
-        ring_x0.step(s)
-        for ring in z1:
-            ring.step(s)
-    ring_x1 = Ring(1, 2, x1)
+            step_all(z1, 0)
+    ring_x0.step(2)
+    step_all(z1, 1)
     ring_x1.step(0)
+    for b in range(2):
+        last[0, b] = finish_z(0, b, z0[b])
+    ring_x0.step(3)
+    step_all(z1, 2)
+    ring_x1.step(1)
+    for b in range(2):
+        close_z(0, b, last[0, b])
+    step_all(z1, 3)
+    ring_x1.step(2)
     close_x(0, ring_x0)
     for b in range(2):
         last[1, b] = finish_z(1, b, z1[b])
-    ring_x1.step(1)
+    ring_x1.step(3)
     for b in range(2):
-        for f in range(2):
-            close_z(f, b, last[f, b])
-    ring_x1.step(2)
-    ring_x1.step(3)
+        close_z(1, b, last[1, b])
     middle(0)
 
-    def spread_near(f, b):
-        return links.send(grads[f].at[pl.ds(2 * b, 1)], grads[f].at[pl.ds(2 * b + 1, 1)], x_far)
-
     class Spread:
-        def __init__(self, f, stream):
-            self.f, self.stream = f, stream
+        def __init__(self, f, place):
+            self.f, self.place = f, place
             self.up = self.down = None
 
         def span(self, dz, first=0, size=2):
-            return self.at(self.f, dz, self.stream * 2 + first, size)
-
-        @staticmethod
-        def at(f, dz, place, size):
-            return grads[f].at[pl.ds((dz % 8) * 8 + place, size)]
+            return grads[self.f].at[pl.ds((dz % 8) * 8 + self.place + first, size)]
 
         def step(self, s):
             if s > 0:
-                self.up.wait_recv()
-                self.down.wait_recv()
+                self.done()
             first, size = ((0, 2), (1, 1))[s == 3]
-            self.up = links.send(
-                self.span(-s, 0, size), self.span(-s - 1, 0, size), z_up
-            )
+            self.up = links.send(self.span(-s, 0, size), self.span(-s - 1, 0, size), z_up)
             self.down = links.send(self.span(s, first, size), self.span(s + 1, first, size), z_down)
 
         def done(self):
             self.up.wait_recv()
             self.down.wait_recv()
 
+    from_twin = {0: [], 1: []}
+    from_far = {}
+
     def to_twin(f, dz, place, size):
-        at = (dz % 8) * 8 + place
-        return links.send(grads[f].at[pl.ds(at, size)], grads[f].at[pl.ds(64 + at, size)], twin)
-
-    def to_far(f, dz):
-        at = (dz % 8) * 8
-        return links.send(grads[f].at[pl.ds(at + 4, 2)], grads[f].at[pl.ds(at + 6, 2)], x_far)
-
-    near = {(f, b): spread_near(f, b) for f in range(2) for b in range(2)}
+        at = dz * 8 + place
+        from_twin[f].append(links.send(grads[f].at[pl.ds(at, size)], grads[f].at[pl.ds(64 + at, size)], twin))
+
+    def to_far(dz, place):
+        at = dz * 8 + place
+        from_far[dz, place] = links.send(grads[0].at[pl.ds(at, 2)], grads[0].at[pl.ds(at + 4, 2)], x_far)
+
+    def near(b):
+        return links.send(grads[1].at[pl.ds(2 * b, 1)], grads[1].at[pl.ds(2 * b + 1, 1)], x_far)
+
+    def around(s):
+        return sorted({-s % 8, s % 8})
+
+    late = [Spread(0, 0), Spread(0, 2)]
+    early = [Spread(1, 2 * b) for b in range(4)]
+
+    def late_round(s):
+        for stream in late:
+            if s < 4:
+                stream.step(s)
+            else:
+                stream.done()
+            for dz in around(s):
+                to_far(dz, stream.place)
+        for dz in around(s):
+            to_twin(0, dz, 0, 4)
+
+    def early_round(s):
+        for b, stream in enumerate(early):
+            if s == 0:
+                nears[b].wait_recv()
+            if s < 4:
+                stream.step(s)
+            else:
+                stream.done()
+            if b % 2:
+                for dz in around(s):
+                    to_twin(1, dz, 4 * (b // 2), 4)
+
+    def far_to_twin(s):
+        for dz in around(s):
+            for place in (0, 2):
+                from_far[dz, place].wait_recv()
+            to_twin(0, dz, 4, 4)
+
+    def all_here(f):
+        for copy in from_twin[f]:
+            copy.wait_recv()
+
+    nears = [near(0), near(1)]
+    late[0].step(0)
+    to_far(0, 0)
     close_x(1, ring_x1)
     middle(1)
-    streams = {f: [Spread(f, 0), Spread(f, 1), Spread(f, 2)] for f in range(2)}
-    from_far = {0: {}, 1: {}}
-    from_twin = {0: [], 1: []}
-
-    def round_of(f, s):
-        for k in (2, 0, 1):
-            if s == 0 and k < 2:
-                near[f, k].wait_recv()
-            if s < 4:
-                streams[f][k].step(s)
-            else:
-                streams[f][k].done()
-            if k == 2:
-                for dz in sorted({-s % 8, s % 8}):
-                    from_far[f][dz] = to_far(f, dz)
-                    from_twin[f].append(to_twin(f, dz, 4, 2))
-        for dz in sorted({-s % 8, s % 8}):
-            from_twin[f].append(to_twin(f, dz, 0, 4))
-
-    def far_to_twin(f, dzs):
-        for dz in dzs:
-            from_far[f][dz % 8].wait_recv()
-            from_twin[f].append(to_twin(f, dz, 6, 2))
-
-    def all_here(f):
-        for copy in from_twin[f]:
-            copy.wait_recv()
+    nears += [near(2), near(3)]
+    late[1].step(0)
+    to_far(0, 2)
+    to_twin(0, 0, 0, 4)
 
     def weight_start():
         def fill(i):
@@ -611,48 +637,55 @@
             [back.at[f, pl.ds(0, 2)]] + [back_y2.at[f, d] for d in (1, 2, 3)],
         )
 
-    round_of(0, 0)
     w_copy = weight_start()
-    round_of(0, 1)
+    late_round(1)
+    early_round(0)
+    late_round(2)
     w_copy = weight_y(w_copy)
-    round_of(0, 2)
-    far_to_twin(0, (0,))
-    round_of(0, 3)
+    late_round(3)
+    early_round(1)
+    far_to_twin(0)
+    far_to_twin(1)
+    late_round(4)
     w_copy = weight_z(w_copy)
-    round_of(1, 0)
-    far_to_twin(0, (1, 7))
-    round_of(0, 4)
-    round_of(1, 1)
+    far_to_twin(2)
+    early_round(2)
     w_copy = weight_x(w_copy)
-    far_to_twin(0, (2, 6))
-    round_of(1, 2)
-    far_to_twin(0, (3, 5, 4))
+    far_to_twin(3)
+    early_round(3)
     w_copy = weight_all_z(w_copy)
+    far_to_twin(4)
     all_here(0)
-    products(0, 0, 2, True)
-    round_of(1, 3)
-    products(0, 1, 2, True)
+    products(0, 0, 1, True)
+    first0 = back_first(0)
+    early_round(4)
     w_copy = weight_all_y(w_copy)
-    first0 = back_first(0)
-    round_of(1, 4)
-    far_to_twin(1, (0, 1, 7, 2, 6))
+    all_here(1)
+    products(1, 0, 2, True)
     second0 = back_second(0, first0)
+    products(1, 1, 2, True)
+    first1 = back_first(1)
     w_copy = weight_all_core(w_copy)
-    far_to_twin(1, (3, 5, 4))
-    all_here(1)
-    products(1, 0, 1, True)
-    first1 = back_first(1)
+    back_third(0, second0)
+    second1 = back_second(1, first1)
     weight_end(w_copy)
-    back_third(0, second0)
-    back_third(1, back_second(1, first1))
+    back_third(1, second1)
     for copy in links.copies:
         copy.wait_send()
+
+
+def finish_kernel(*refs):
+    copies = [pltpu.make_async_copy(refs[i], refs[3 + i], refs[6].at[i]) for i in range(3)]
+    for copy in copies:
+        copy.start()
+    for copy in copies:
+        copy.wait()
 
 
 def per_device(features, weight, cotangent, tile_rows, tile_cols, tile_values, tile_count):
     table = pl.pallas_call(
         order_kernel,
-        out_shape=jax.ShapeDtypeStruct((8, T), jnp.int32),
+        out_shape=jax.ShapeDtypeStruct((LINES, T), jnp.int32),
         in_specs=[
             pl.BlockSpec(memory_space=pltpu.SMEM),
             pl.BlockSpec(memory_space=pltpu.VMEM),
@@ -669,13 +702,14 @@
     def pieces(*counts):
         return pltpu.VMEM((*counts, 8, 128), F32)
 
+    out_shape = (
+        jax.ShapeDtypeStruct((4, T, 256), BF16),
+        jax.ShapeDtypeStruct((4, T, 256), BF16),
+        jax.ShapeDtypeStruct((256, 256), F32),
+    )
     hidden, grad_feat, grad_weight = pl.pallas_call(
         layer_kernel,
-        out_shape=(
-            jax.ShapeDtypeStruct((4, T, 256), BF16),
-            jax.ShapeDtypeStruct((4, T, 256), BF16),
-            jax.ShapeDtypeStruct((256, 256), F32),
-        ),
+        out_shape=out_shape,
         in_specs=[pl.BlockSpec(memory_space=pltpu.SMEM), hbm, vmem, hbm, hbm],
         out_specs=(vmem, vmem, vmem),
         scratch_shapes=[
@@ -725,6 +759,14 @@
         cotangent.reshape(4, T, 256),
         tile_values.reshape(T, T, T),
     )
+    hidden, grad_feat, grad_weight = pl.pallas_call(
+        finish_kernel,
+        out_shape=out_shape,
+        in_specs=[hbm] * 3,
+        out_specs=[vmem] * 3,
+        scratch_shapes=[pltpu.SemaphoreType.DMA((3,))],
+        name="finish",
+    )(hidden, grad_feat, grad_weight)
     return hidden.reshape(4 * T, 256), grad_feat.reshape(4 * T, 256), grad_weight
 
 

time: 153 us -> 140 us (0.915)
  Pallas kernels: 146 us -> 139 us
  local copies, waits for them, and re-layouts: 5.01 us -> 0 us
    pallas_call x2 -> x3, Pallas kernels: 146 us -> 139 us  [the longest x1 135 us: per_device(): pl.pallas_call(layer_kernel, out_shape=out_shape, in_specs=[pl.BlockSpec(...]
    unnamed x3 -> x0, local copies, waits for them, and re-layouts: 5.01 us -> none
where the time goes in v2:
time: 140 us
  Pallas kernels  139 us (99%)
    pallas_call x1, Pallas kernels, per_device(): pl.pallas_call(layer_kernel, out_shape=out_shape, in_specs=[pl.BlockSpec(...  135 us

profile of v2, /device:TPU:1, one launch (start us, length us, event | category | flops | bytes accessed | tf_op | source)
XLA Modules:
  0.0 139.9 jit_solution(7660076997389573390)
XLA Ops:
  1.3 1.9 %order.1.table = s32[9,128]{1,0:T(8,128)} custom-call(s32[1,1]{1,0:T(1,128)S(6)} %copy.10.count_ref, s32[1,128]{1,0:T(1,128)} %bitcast.7, s32[1,128]{1,0:T(1,128)} %bitcast.8), custom_call_target="tpu_custom_call" | custom-call | tf_op jit(solution)/shard_map/order/pallas_call | solution.py:686
  3.2 134.7 %layer.1 = (bf16[4,128,256]{2,1,0:T(8,128)(2,1)}, bf16[4,128,256]{2,1,0:T(8,128)(2,1)}, f32[256,256]{1,0:T(8,128)}) custom-call(s32[9,128]{1,0:T(8,128)} %order.1.table, bf16[4,128,256]{2,1,0:T(8,128)(2,1)} %bitcast.10, bf16[256,256]{1,0:T(8,128)(2,1)} %weight.1, bf16[4,128,256]{2,1,0:T(8,128)(2,1)} %bitcast.11, bf16[128,128,128]{2,1,0:T(8,128)(2,1)} %bitcast.9), custom_call_target="tpu_custom_call" | custom-call | flops 5000000000 | bytes 6291456 | tf_op jit(solution)/shard_map/layer/pallas_call | solution.py:710
  137.9 2.0 %finish.1 = (bf16[4,128,256]{2,1,0:T(8,128)(2,1)}, bf16[4,128,256]{2,1,0:T(8,128)(2,1)}, f32[256,256]{1,0:T(8,128)}) custom-call(bf16[4,128,256]{2,1,0:T(8,128)(2,1)} %get-tuple-element.9.refs_0_, bf16[4,128,256]{2,1,0:T(8,128)(2,1)} %get-tuple-element.10.refs_1_, f32[256,256]{1,0:T(8,128)} %get-tuple-element.11.refs_2_), custom_call_target="tpu_custom_call" | custom-call | tf_op jit(solution)/shard_map/finish/pallas_call | solution.py:762

commit v3 on v2

--- a/solution.py
+++ b/solution.py
@@ -13,7 +13,7 @@
 T = 128
 HALF = 128
 COPIES = 340
-GROUP = 8
+GROUP = 32
 URGENT = (4, 3, 5, 2, 6, 1, 7, 0)
 
 
@@ -34,25 +34,22 @@
 
 
 ROW_TILE, ROW_KEEP, ROW_LAST, ROW_FEAT, COL_TILE, COL_KEEP, COL_LAST, COL_GRAD = range(8)
-LINES = 9
-
-
-def order_kernel(count_ref, rows_ref, cols_ref, table_ref):
-    here = position()
+LINES = 16
+
+
+def fill_table(here, count, rows, cols, table_ref):
     lane = lax.broadcasted_iota(jnp.int32, (T, T), 1)
     sub = lax.broadcasted_iota(jnp.int32, (T, T), 0)
     eye = lane == sub
-    count = count_ref[0, 0]
 
     def spread(values):
         return jnp.broadcast_to(values, (T, T))
 
     def column(values):
-        kept = jnp.where(eye, spread(values), 0).astype(F32)
-        return jnp.broadcast_to(jnp.sum(kept, axis=1, keepdims=True), (T, T)).astype(jnp.int32)
+        return jnp.broadcast_to(jnp.sum(jnp.where(eye, spread(values), 0), axis=1, keepdims=True), (T, T))
 
     def total(values):
-        return jnp.sum(values.astype(F32), axis=0, keepdims=True).astype(jnp.int32)
+        return jnp.sum(values, axis=0, keepdims=True)
 
     live_down = sub < count
 
@@ -76,7 +73,6 @@
     def far_first(block, x_other):
         return 2 * block + x_other
 
-    rows, cols = rows_ref[...], cols_ref[...]
     rows_down, cols_down = column(rows), feat_place(column(cols))
     grads_down = [row_place(rows_down, far_last), row_place(rows_down, far_first)]
     rows_down = row_place(rows_down, sum_order)
@@ -86,8 +82,8 @@
         big = T * T
         key = jnp.where(lane < count, spread(keys) * T + lane, big + lane)
         key_down = jnp.where(live_down, keys_down * T + sub, big + sub)
-        rank_down = jnp.sum((key < key_down).astype(F32), axis=1, keepdims=True)
-        rank_down = jnp.broadcast_to(rank_down, (T, T)).astype(jnp.int32)
+        rank_down = jnp.sum(jnp.where(key < key_down, 1, 0), axis=1, keepdims=True)
+        rank_down = jnp.broadcast_to(rank_down, (T, T))
         now = rank_down == lane
         tile = total(jnp.where(now, sub, 0))
         values = [total(jnp.where(now, value, 0)) for value in values_down]
@@ -100,6 +96,7 @@
         return [tile, keep, jnp.where(some > 0, upto - 1, T), *values]
 
     lines = sorted_by(rows, rows_down, [cols_down]) + sorted_by(cols, cols_down, grads_down)
+    table_ref[...] = jnp.zeros_like(table_ref)
     for number, line in enumerate(lines):
         table_ref[number : number + 1, :] = line
 
@@ -143,14 +140,21 @@
 
 
 def layer_kernel(
-    table,
+    count,
+    rows_hbm,
+    cols_hbm,
     feat_hbm,
-    weight,
+    weight_hbm,
     cot_hbm,
     tile_hbm,
     hidden,
     grad_feat,
     grad_weight,
+    table,
+    lines,
+    rows_in,
+    cols_in,
+    weight,
     tiles,
     cot,
     feats0,
@@ -195,27 +199,28 @@
     y_to = {d: device(here, y=d) for d in (1, 2, 3)}
     z_to = {d: device(here, z=d) for d in range(1, 8)}
 
-    loads = [
-        pltpu.make_async_copy(feat_hbm.at[:, :, pl.ds(f * HALF, HALF)], feats[f].at[pl.ds(0, 4)], local_sem.at[f])
-        for f in range(2)
+    feat_own = [feat_hbm.at[:, :, pl.ds(f * HALF, HALF)] for f in range(2)]
+    moves = [
+        (rows_hbm, rows_in),
+        (cols_hbm, cols_in),
+        (feat_own[0], feats[0].at[pl.ds(0, 4)]),
+        (feat_own[1], feats[1].at[pl.ds(0, 4)]),
+        (tile_hbm, tiles),
+        (weight_hbm, weight),
+        (cot_hbm, cot),
     ]
-    loads.append(pltpu.make_async_copy(tile_hbm, tiles, local_sem.at[2]))
-    loads.append(pltpu.make_async_copy(cot_hbm, cot, local_sem.at[3]))
+    loads = [pltpu.make_async_copy(src, dst, local_sem.at[i]) for i, (src, dst) in enumerate(moves)]
     for load in loads:
         load.start()
 
     barrier = pltpu.get_barrier_semaphore()
-    partners = [x_far, x_near, x_both, twin, *y_to.values(), *z_to.values()]
+    partners = [x_far, x_near, twin, z_up, z_down, *y_to.values()]
     for partner in partners:
         pl.semaphore_signal(barrier, inc=1, device_id=partner, device_id_type=MESH)
-    for f in range(2):
-        slots[f, T] = jnp.zeros((T, HALF), BF16)
-    loads[0].wait()
-    loads[1].wait()
     pl.semaphore_wait(barrier, len(partners))
 
     def gather_first(f):
-        own = feats[f].at[pl.ds(0, 4)]
+        own = feat_own[f]
         near = links.send(own, feats[f].at[pl.ds(16, 4)], x_near)
         over = {d: links.send(own, feats[f].at[pl.ds((4 - d) * 4, 4)], y_to[d]) for d in (1, 3, 2)}
         return near, over
@@ -364,10 +369,18 @@
         each(2, body)
 
     first = gather_first(0)
+    loads[0].wait()
+    loads[1].wait()
+    fill_table(here, count[0, 0], rows_in[...], cols_in[...], lines)
+    table_copy = pltpu.make_async_copy(lines, table, local_sem.at[7])
+    table_copy.start()
+    for load in loads[2:]:
+        load.wait()
     second = gather_second(0, first)
     first1 = gather_first(1)
-    loads[2].wait()
-    loads[3].wait()
+    table_copy.wait()
+    for f in range(2):
+        slots[f, T] = jnp.zeros((T, HALF), BF16)
     w_sum[...] = jnp.zeros_like(w_sum)
     carry[...] = jnp.zeros_like(carry)
     for copy in second:
@@ -683,17 +696,6 @@
 
 
 def per_device(features, weight, cotangent, tile_rows, tile_cols, tile_values, tile_count):
-    table = pl.pallas_call(
-        order_kernel,
-        out_shape=jax.ShapeDtypeStruct((LINES, T), jnp.int32),
-        in_specs=[
-            pl.BlockSpec(memory_space=pltpu.SMEM),
-            pl.BlockSpec(memory_space=pltpu.VMEM),
-            pl.BlockSpec(memory_space=pltpu.VMEM),
-        ],
-        out_specs=pl.BlockSpec(memory_space=pltpu.VMEM),
-        name="order",
-    )(tile_count, tile_rows.reshape(1, T), tile_cols.reshape(1, T))
     hbm, vmem = pl.BlockSpec(memory_space=pl.ANY), pl.BlockSpec(memory_space=pltpu.VMEM)
 
     def blocks(*counts):
@@ -710,9 +712,14 @@
     hidden, grad_feat, grad_weight = pl.pallas_call(
         layer_kernel,
         out_shape=out_shape,
-        in_specs=[pl.BlockSpec(memory_space=pltpu.SMEM), hbm, vmem, hbm, hbm],
+        in_specs=[pl.BlockSpec(memory_space=pltpu.SMEM)] + [hbm] * 6,
         out_specs=(vmem, vmem, vmem),
         scratch_shapes=[
+            pltpu.SMEM((LINES, T), jnp.int32),
+            pltpu.VMEM((LINES, T), jnp.int32),
+            pltpu.VMEM((1, T), jnp.int32),
+            pltpu.VMEM((1, T), jnp.int32),
+            pltpu.VMEM((256, 256), BF16),
             blocks(T),
             pltpu.VMEM((4, T, 256), BF16),
             blocks(32),
@@ -743,7 +750,7 @@
             pieces(8),
             pieces(32),
             pieces(64),
-            pltpu.SemaphoreType.DMA((4,)),
+            pltpu.SemaphoreType.DMA((8,)),
             pltpu.SemaphoreType.DMA((COPIES,)),
             pltpu.SemaphoreType.DMA((COPIES,)),
         ],
@@ -753,7 +760,9 @@
         cost_estimate=pl.CostEstimate(flops=5 * 10**9, bytes_accessed=6 * 2**20, transcendentals=2**17),
         name="layer",
     )(
-        table,
+        tile_count,
+        tile_rows.reshape(1, T),
+        tile_cols.reshape(1, T),
         features.reshape(4, T, 256),
         weight,
         cotangent.reshape(4, T, 256),

time: 140 us -> 131 us (0.936)
  Pallas kernels: 139 us -> 130 us
    pallas_call x1, Pallas kernels: 135 us -> 128 us  [per_device(): pl.pallas_call(layer_kernel, out_shape=out_shape, in_specs=[pl.BlockSpec(...]
    pallas_call x1 -> x0, Pallas kernels: 1.91 us -> none  [per_device(): pl.pallas_call(order_kernel, out_shape=jax.ShapeDtypeStruct((LINES, T), j...]
where the time goes in v3:
time: 131 us
  Pallas kernels  130 us (99%)
    pallas_call x1, Pallas kernels, per_device(): pl.pallas_call(layer_kernel, out_shape=out_shape, in_specs=[pl.BlockSpec(...  128 us

profile of v3, /device:TPU:1, one launch (start us, length us, event | category | flops | bytes accessed | tf_op | source)
XLA Modules:
  0.0 131.0 jit_solution(15870852720587310899)
XLA Ops:
  1.3 127.7 %layer.1 = (bf16[4,128,256]{2,1,0:T(8,128)(2,1)}, bf16[4,128,256]{2,1,0:T(8,128)(2,1)}, f32[256,256]{1,0:T(8,128)}) custom-call(s32[1,1]{1,0:T(1,128)S(6)} %copy.10.count, s32[1,128]{1,0:T(1,128)} %bitcast.12, s32[1,128]{1,0:T(1,128)} %bitcast.13, bf16[4,128,256]{2,1,0:T(8,128)(2,1)} %bitcast.8, bf16[256,256]{1,0:T(8,128)(2,1)} %weight_hbm.1, ...), custom_call_target="tpu_custom_call" | custom-call | flops 5000000000 | bytes 6291456 | tf_op jit(solution)/shard_map/layer/pallas_call | solution.py:712
  129.0 2.0 %finish.1 = (bf16[4,128,256]{2,1,0:T(8,128)(2,1)}, bf16[4,128,256]{2,1,0:T(8,128)(2,1)}, f32[256,256]{1,0:T(8,128)}) custom-call(bf16[4,128,256]{2,1,0:T(8,128)(2,1)} %get-tuple-element.9.refs_0_, bf16[4,128,256]{2,1,0:T(8,128)(2,1)} %get-tuple-element.10.refs_1_, f32[256,256]{1,0:T(8,128)} %get-tuple-element.11.refs_2_), custom_call_target="tpu_custom_call" | custom-call | tf_op jit(solution)/shard_map/finish/pallas_call | solution.py:771

commit v4 on v3

--- a/solution.py
+++ b/solution.py
@@ -140,7 +140,7 @@
 
 
 def layer_kernel(
-    count,
+    count_hbm,
     rows_hbm,
     cols_hbm,
     feat_hbm,
@@ -152,6 +152,7 @@
     grad_weight,
     table,
     lines,
+    count,
     rows_in,
     cols_in,
     weight,
@@ -208,6 +209,7 @@
         (tile_hbm, tiles),
         (weight_hbm, weight),
         (cot_hbm, cot),
+        (count_hbm, count),
     ]
     loads = [pltpu.make_async_copy(src, dst, local_sem.at[i]) for i, (src, dst) in enumerate(moves)]
     for load in loads:
@@ -220,20 +222,30 @@
     pl.semaphore_wait(barrier, len(partners))
 
     def gather_first(f):
-        own = feat_own[f]
-        near = links.send(own, feats[f].at[pl.ds(16, 4)], x_near)
-        over = {d: links.send(own, feats[f].at[pl.ds((4 - d) * 4, 4)], y_to[d]) for d in (1, 3, 2)}
+        own = [feat_own[f].at[pl.ds(b, 2)] for b in (0, 2)]
+        near = [links.send(own[i], feats[f].at[pl.ds(16 + 2 * i, 2)], x_near) for i in range(2)]
+        over = [
+            {d: links.send(own[i], feats[f].at[pl.ds((4 - d) * 4 + 2 * i, 2)], y_to[d]) for d in (2, 1, 3)}
+            for i in (1, 0)
+        ]
         return near, over
 
-    def gather_second(f, first):
-        near, over = first
-        near.wait_recv()
-        copies = [
-            links.send(feats[f].at[pl.ds(16, 2)], feats[f].at[pl.ds(16 + (4 - d) * 4, 2)], y_to[d])
-            for d in (1, 3, 2)
+    def gather_y(f, first):
+        near, _ = first
+        size = 4 if f else 2
+        near[0].wait_recv()
+        if f:
+            near[1].wait_recv()
+        return [
+            links.send(feats[f].at[pl.ds(16, size)], feats[f].at[pl.ds(16 + (4 - d) * 4, size)], y_to[d])
+            for d in (2, 1, 3)
         ]
+
+    def gather_x(f, first):
+        near, (late_over, over) = first
+        copies = [near[1], *over.values()]
         for d in (1, 3, 2):
-            over[d].wait_recv()
+            late_over[d].wait_recv()
             rows = (4 - d) * 4 + 2
             copies.append(links.send(feats[f].at[pl.ds(rows, 2)], feats[f].at[pl.ds(16 + rows, 2)], x_near))
         return copies
@@ -369,14 +381,14 @@
         each(2, body)
 
     first = gather_first(0)
-    loads[0].wait()
-    loads[1].wait()
+    for load in (loads[0], loads[1], loads[7]):
+        load.wait()
     fill_table(here, count[0, 0], rows_in[...], cols_in[...], lines)
-    table_copy = pltpu.make_async_copy(lines, table, local_sem.at[7])
+    table_copy = pltpu.make_async_copy(lines, table, local_sem.at[8])
     table_copy.start()
-    for load in loads[2:]:
+    for load in loads[2:7]:
         load.wait()
-    second = gather_second(0, first)
+    second = gather_y(0, first) + gather_x(0, first)
     first1 = gather_first(1)
     table_copy.wait()
     for f in range(2):
@@ -387,7 +399,9 @@
         copy.wait_recv()
     products(0, 0, 1, False)
     core0 = core_send(0)
-    second1 = gather_second(1, first1)
+    second1 = gather_y(1, first1)
+    for over in first1[1]:
+        second1 += over.values()
     x0, x1, last = {}, {}, {}
     z0 = [Ring(0, 0), Ring(0, 1)]
     z1 = [Ring(1, 0), Ring(1, 1)]
@@ -653,20 +667,20 @@
     w_copy = weight_start()
     late_round(1)
     early_round(0)
+    w_copy = weight_y(w_copy)
     late_round(2)
-    w_copy = weight_y(w_copy)
+    early_round(1)
     late_round(3)
-    early_round(1)
+    w_copy = weight_z(w_copy)
     far_to_twin(0)
     far_to_twin(1)
+    early_round(2)
     late_round(4)
-    w_copy = weight_z(w_copy)
+    w_copy = weight_x(w_copy)
     far_to_twin(2)
-    early_round(2)
-    w_copy = weight_x(w_copy)
-    far_to_twin(3)
     early_round(3)
     w_copy = weight_all_z(w_copy)
+    far_to_twin(3)
     far_to_twin(4)
     all_here(0)
     products(0, 0, 1, True)
@@ -712,11 +726,12 @@
     hidden, grad_feat, grad_weight = pl.pallas_call(
         layer_kernel,
         out_shape=out_shape,
-        in_specs=[pl.BlockSpec(memory_space=pltpu.SMEM)] + [hbm] * 6,
+        in_specs=[hbm] * 7,
         out_specs=(vmem, vmem, vmem),
         scratch_shapes=[
             pltpu.SMEM((LINES, T), jnp.int32),
             pltpu.VMEM((LINES, T), jnp.int32),
+            pltpu.SMEM((1, 1), jnp.int32),
             pltpu.VMEM((1, T), jnp.int32),
             pltpu.VMEM((1, T), jnp.int32),
             pltpu.VMEM((256, 256), BF16),
@@ -750,7 +765,7 @@
             pieces(8),
             pieces(32),
             pieces(64),
-            pltpu.SemaphoreType.DMA((8,)),
+            pltpu.SemaphoreType.DMA((9,)),
             pltpu.SemaphoreType.DMA((COPIES,)),
             pltpu.SemaphoreType.DMA((COPIES,)),
         ],

time: 131 us -> 128 us (0.977)
  Pallas kernels: 130 us -> 127 us
    pallas_call x1, Pallas kernels: 128 us -> 125 us  [per_device(): pl.pallas_call(layer_kernel, out_shape=out_shape, in_specs=[hbm] * 7, out...]
where the time goes in v4:
time: 128 us
  Pallas kernels  127 us (99%)
  between operations  1.29 us (1%)
    pallas_call x1, Pallas kernels, per_device(): pl.pallas_call(layer_kernel, out_shape=out_shape, in_specs=[hbm] * 7, out...  125 us

profile of v4, /device:TPU:1, one launch (start us, length us, event | category | flops | bytes accessed | tf_op | source)
XLA Modules:
  0.0 128.1 jit_solution(15355449367819263192)
XLA Ops:
  1.3 124.8 %layer.1 = (bf16[4,128,256]{2,1,0:T(8,128)(2,1)}, bf16[4,128,256]{2,1,0:T(8,128)(2,1)}, f32[256,256]{1,0:T(8,128)}) custom-call(s32[1,1]{1,0:T(1,128)S(6)} %copy.10.count_hbm, s32[1,128]{1,0:T(1,128)} %bitcast.12, s32[1,128]{1,0:T(1,128)} %bitcast.13, bf16[4,128,256]{2,1,0:T(8,128)(2,1)} %bitcast.8, bf16[256,256]{1,0:T(8,128)(2,1)} %weight_hbm.1, ...), custom_call_target="tpu_custom_call" | custom-call | flops 5000000000 | bytes 6291456 | tf_op jit(solution)/shard_map/layer/pallas_call | solution.py:726
  126.1 2.0 %finish.1 = (bf16[4,128,256]{2,1,0:T(8,128)(2,1)}, bf16[4,128,256]{2,1,0:T(8,128)(2,1)}, f32[256,256]{1,0:T(8,128)}) custom-call(bf16[4,128,256]{2,1,0:T(8,128)(2,1)} %get-tuple-element.9.refs_0_, bf16[4,128,256]{2,1,0:T(8,128)(2,1)} %get-tuple-element.10.refs_1_, f32[256,256]{1,0:T(8,128)} %get-tuple-element.11.refs_2_), custom_call_target="tpu_custom_call" | custom-call | tf_op jit(solution)/shard_map/finish/pallas_call | solution.py:786

commit v5 on v4

--- a/solution.py
+++ b/solution.py
@@ -13,7 +13,7 @@
 T = 128
 HALF = 128
 COPIES = 340
-GROUP = 32
+GROUP = 64
 URGENT = (4, 3, 5, 2, 6, 1, 7, 0)
 
 
@@ -221,34 +221,52 @@
         pl.semaphore_signal(barrier, inc=1, device_id=partner, device_id_type=MESH)
     pl.semaphore_wait(barrier, len(partners))
 
-    def gather_first(f):
-        own = [feat_own[f].at[pl.ds(b, 2)] for b in (0, 2)]
-        near = [links.send(own[i], feats[f].at[pl.ds(16 + 2 * i, 2)], x_near) for i in range(2)]
-        over = [
-            {d: links.send(own[i], feats[f].at[pl.ds((4 - d) * 4 + 2 * i, 2)], y_to[d]) for d in (2, 1, 3)}
-            for i in (1, 0)
-        ]
-        return near, over
-
-    def gather_y(f, first):
-        near, _ = first
-        size = 4 if f else 2
+    def over(f, src, place, size=2):
+        return {d: links.send(src, feats[f].at[pl.ds((4 - d) * 4 + place, size)], y_to[d]) for d in (1, 3)}
+
+    def relay(f, copies, place, size=1):
+        sent = []
+        for d, group, first in ((1, 12, 0), (3, 4, size)):
+            copies[d].wait_recv()
+            src = feats[f].at[pl.ds(group + place + first, size)]
+            sent.append(links.send(src, feats[f].at[pl.ds(8 + place + first, size)], y_to[d]))
+        return sent
+
+    def across(f, group):
+        rows = group * 4 + 2
+        return links.send(feats[f].at[pl.ds(rows, 2)], feats[f].at[pl.ds(16 + rows, 2)], x_near)
+
+    def gather_mixed():
+        own = [feat_own[0].at[pl.ds(b, 2)] for b in (0, 2)]
+        near = [links.send(own[0], feats[0].at[pl.ds(16, 2)], x_near)]
+        late = over(0, own[1], 2)
+        near.append(links.send(own[1], feats[0].at[pl.ds(18, 2)], x_near))
+        return near, late, over(0, own[0], 0)
+
+    def gather_rest(first):
+        near, late, early = first
+        late_two = relay(0, late, 2)
+        copies = [near[1], across(0, 3), across(0, 1)]
         near[0].wait_recv()
-        if f:
-            near[1].wait_recv()
-        return [
-            links.send(feats[f].at[pl.ds(16, size)], feats[f].at[pl.ds(16 + (4 - d) * 4, size)], y_to[d])
+        near_over = over(0, feats[0].at[pl.ds(16, 2)], 16)
+        copies += relay(0, early, 0)
+        for copy in late_two:
+            copy.wait_recv()
+        copies.append(across(0, 2))
+        return copies + relay(0, near_over, 16)
+
+    def gather_plain():
+        own = feat_own[1]
+        copies = [links.send(own, feats[1].at[pl.ds((4 - d) * 4, 4)], y_to[d]) for d in (2, 1, 3)]
+        return links.send(own, feats[1].at[pl.ds(16, 4)], x_near), copies
+
+    def gather_near(first):
+        near, copies = first
+        near.wait_recv()
+        return copies + [
+            links.send(feats[1].at[pl.ds(16, 4)], feats[1].at[pl.ds(16 + (4 - d) * 4, 4)], y_to[d])
             for d in (2, 1, 3)
         ]
-
-    def gather_x(f, first):
-        near, (late_over, over) = first
-        copies = [near[1], *over.values()]
-        for d in (1, 3, 2):
-            late_over[d].wait_recv()
-            rows = (4 - d) * 4 + 2
-            copies.append(links.send(feats[f].at[pl.ds(rows, 2)], feats[f].at[pl.ds(16 + rows, 2)], x_near))
-        return copies
 
     def products(f, piece, pieces, back_pass):
         tile_line, value_line, keep_line = (
@@ -380,7 +398,7 @@
 
         each(2, body)
 
-    first = gather_first(0)
+    first = gather_mixed()
     for load in (loads[0], loads[1], loads[7]):
         load.wait()
     fill_table(here, count[0, 0], rows_in[...], cols_in[...], lines)
@@ -388,8 +406,8 @@
     table_copy.start()
     for load in loads[2:7]:
         load.wait()
-    second = gather_y(0, first) + gather_x(0, first)
-    first1 = gather_first(1)
+    second = gather_rest(first)
+    first1 = gather_plain()
     table_copy.wait()
     for f in range(2):
         slots[f, T] = jnp.zeros((T, HALF), BF16)
@@ -399,9 +417,7 @@
         copy.wait_recv()
     products(0, 0, 1, False)
     core0 = core_send(0)
-    second1 = gather_y(1, first1)
-    for over in first1[1]:
-        second1 += over.values()
+    second1 = gather_near(first1)
     x0, x1, last = {}, {}, {}
     z0 = [Ring(0, 0), Ring(0, 1)]
     z1 = [Ring(1, 0), Ring(1, 1)]

time: 128 us -> 127 us (level)
  no operation moved by 1% of the time
where the time goes in v5:
time: 127 us
  Pallas kernels  126 us (99%)
  between operations  1.29 us (1%)
    pallas_call x1, Pallas kernels, per_device(): pl.pallas_call(layer_kernel, out_shape=out_shape, in_specs=[hbm] * 7, out...  124 us

profile of v5, /device:TPU:1, one launch (start us, length us, event | category | flops | bytes accessed | tf_op | source)
XLA Modules:
  0.0 127.3 jit_solution(11957501400774914733)
XLA Ops:
  1.3 124.0 %layer.1 = (bf16[4,128,256]{2,1,0:T(8,128)(2,1)}, bf16[4,128,256]{2,1,0:T(8,128)(2,1)}, f32[256,256]{1,0:T(8,128)}) custom-call(s32[1,1]{1,0:T(1,128)S(6)} %copy.10.count_hbm, s32[1,128]{1,0:T(1,128)} %bitcast.12, s32[1,128]{1,0:T(1,128)} %bitcast.13, bf16[4,128,256]{2,1,0:T(8,128)(2,1)} %bitcast.8, bf16[256,256]{1,0:T(8,128)(2,1)} %weight_hbm.1, ...), custom_call_target="tpu_custom_call" | custom-call | flops 5000000000 | bytes 6291456 | tf_op jit(solution)/shard_map/layer/pallas_call | solution.py:742
  125.3 2.0 %finish.1 = (bf16[4,128,256]{2,1,0:T(8,128)(2,1)}, bf16[4,128,256]{2,1,0:T(8,128)(2,1)}, f32[256,256]{1,0:T(8,128)}) custom-call(bf16[4,128,256]{2,1,0:T(8,128)(2,1)} %get-tuple-element.9.refs_0_, bf16[4,128,256]{2,1,0:T(8,128)(2,1)} %get-tuple-element.10.refs_1_, f32[256,256]{1,0:T(8,128)} %get-tuple-element.11.refs_2_), custom_call_target="tpu_custom_call" | custom-call | tf_op jit(solution)/shard_map/finish/pallas_call | solution.py:802

commit v6 on v5

--- a/solution.py
+++ b/solution.py
@@ -404,10 +404,10 @@
     fill_table(here, count[0, 0], rows_in[...], cols_in[...], lines)
     table_copy = pltpu.make_async_copy(lines, table, local_sem.at[8])
     table_copy.start()
+    second = gather_rest(first)
+    first1 = gather_plain()
     for load in loads[2:7]:
         load.wait()
-    second = gather_rest(first)
-    first1 = gather_plain()
     table_copy.wait()
     for f in range(2):
         slots[f, T] = jnp.zeros((T, HALF), BF16)
@@ -698,10 +698,10 @@
     w_copy = weight_all_z(w_copy)
     far_to_twin(3)
     far_to_twin(4)
+    early_round(4)
     all_here(0)
     products(0, 0, 1, True)
     first0 = back_first(0)
-    early_round(4)
     w_copy = weight_all_y(w_copy)
     all_here(1)
     products(1, 0, 2, True)

time: 127 us -> 127 us (level)
  no operation moved by 1% of the time
where the time goes in v6:
time: 127 us
  Pallas kernels  126 us (99%)
  between operations  1.29 us (1%)
    pallas_call x1, Pallas kernels, per_device(): pl.pallas_call(layer_kernel, out_shape=out_shape, in_specs=[hbm] * 7, out...  124 us

profile of v6, /device:TPU:1, one launch (start us, length us, event | category | flops | bytes accessed | tf_op | source)
XLA Modules:
  0.0 127.1 jit_solution(18041871621947844214)
XLA Ops:
  1.3 123.8 %layer.1 = (bf16[4,128,256]{2,1,0:T(8,128)(2,1)}, bf16[4,128,256]{2,1,0:T(8,128)(2,1)}, f32[256,256]{1,0:T(8,128)}) custom-call(s32[1,1]{1,0:T(1,128)S(6)} %copy.10.count_hbm, s32[1,128]{1,0:T(1,128)} %bitcast.12, s32[1,128]{1,0:T(1,128)} %bitcast.13, bf16[4,128,256]{2,1,0:T(8,128)(2,1)} %bitcast.8, bf16[256,256]{1,0:T(8,128)(2,1)} %weight_hbm.1, ...), custom_call_target="tpu_custom_call" | custom-call | flops 5000000000 | bytes 6291456 | tf_op jit(solution)/shard_map/layer/pallas_call | solution.py:742
  125.1 2.0 %finish.1 = (bf16[4,128,256]{2,1,0:T(8,128)(2,1)}, bf16[4,128,256]{2,1,0:T(8,128)(2,1)}, f32[256,256]{1,0:T(8,128)}) custom-call(bf16[4,128,256]{2,1,0:T(8,128)(2,1)} %get-tuple-element.9.refs_0_, bf16[4,128,256]{2,1,0:T(8,128)(2,1)} %get-tuple-element.10.refs_1_, f32[256,256]{1,0:T(8,128)} %get-tuple-element.11.refs_2_), custom_call_target="tpu_custom_call" | custom-call | tf_op jit(solution)/shard_map/finish/pallas_call | solution.py:802
